TPU v7x, 32 devices: a whole 2x2x4 slice. The times are simulated.
32 devices in a mesh: group: 2 (over y), dm: 4 (over z), tm: 2 (over x), beam: 2 (over core).
Axes of the slice: x: 2, y: 2, z: 4, core: 2. Of those that a mesh axis runs over, the one named last changes fastest.
Arguments:
- raw: bfloat16 [16, 4194304], P(('group', 'dm', 'beam'), 'tm'), parts along dimension 0
- proto: float32 [4, 16384], replicated, may hold values from -4 to 4
- delays: int32 [8, 4, 64], replicated, may hold values from 0 to 3, as said below
- widths: int32 [8], replicated, may hold values from 1 to 8, as said below
- owners: int32 [8, 1], replicated, may hold values from 0 to 3; in each aligned block of 8 rows (0 to 7, 8 to 15, ...) at most 4 rows name the same one
Outputs:
- detect: bfloat16 [16, 8, 2, 4, 8, 256], P('dm', 'group', 'beam', None, None, 'tm'), parts along dimension 1
There are 2 independent parts, one for each index of `group`. A program takes and returns all parts, laid end to end along the dimension named above; an argument that names none is the same for every part. Nothing has to cross between parts.
Inputs may be any that keep to these rules, and one draw needn't show every extreme that they name: `delays`: 3 occurs in every draw. `widths`: 8 occurs in every draw. `owners`: each owner holds at most 4 DM blocks, and some owner holds exactly 4.
All inputs are finite; a program needn't handle non-finite values.
Results may differ from a plain program's by a relative error of at most 0.014.
Values may be sent and summed in bfloat16 or wider, within the bound.
A program may use at most 128 MiB of HBM per device.

v0:
```python
import math
import jax
import jax.numpy as jnp
from jax import lax
from jax.sharding import PartitionSpec as P

DFT_A = 128
NBLK = 64
PFB_BLK = 16
FD = 4
TT = 8
MAXT = 3
WMAX = 8


def shifted(value, axis, steps):
    count = lax.axis_size(axis)
    first, last = (max(0, -steps), min(count, count - steps))
    return lax.ppermute(value, axis, [(source, source + steps) for source in range(first, last)])


def dft_tables(size):
    index = jnp.arange(size, dtype=jnp.int32)
    product = index[:, None] * index[None, :] % size
    angle = product.astype(jnp.float32) * (2.0 * math.pi / size)
    return (jnp.cos(angle).astype(jnp.bfloat16), jnp.sin(angle).astype(jnp.bfloat16))


def twiddle_tables(rows, cols, total):
    first = jnp.arange(rows, dtype=jnp.int32)
    second = jnp.arange(cols, dtype=jnp.int32)
    product = first[:, None] * second[None, :] % total
    angle = product.astype(jnp.float32) * (2.0 * math.pi / total)
    return (jnp.cos(angle), jnp.sin(angle))


def spectra_power(window_frames, proto):
    taps, channels = proto.shape
    beams_here = window_frames.shape[0]
    count = window_frames.shape[1] - taps + 1
    side_b = channels // DFT_A
    acc = window_frames[:, 0:count].astype(jnp.float32) * proto[0]
    for tap in range(1, taps):
        acc = acc + window_frames[:, tap : tap + count].astype(jnp.float32) * proto[tap]
    frames_bf = acc.astype(jnp.bfloat16).reshape(beams_here * count, DFT_A, side_b)
    cos_a, sin_a = dft_tables(DFT_A)
    cos_b, sin_b = dft_tables(side_b)
    tw_cos, tw_sin = twiddle_tables(side_b, DFT_A, channels)
    a_re = jnp.einsum("kab,fa->kbf", frames_bf, cos_a, preferred_element_type=jnp.float32)
    a_im = -jnp.einsum("kab,fa->kbf", frames_bf, sin_a, preferred_element_type=jnp.float32)
    t_re = (a_re * tw_cos + a_im * tw_sin).astype(jnp.bfloat16)
    t_im = (a_im * tw_cos - a_re * tw_sin).astype(jnp.bfloat16)
    c_re = jnp.einsum("kbf,gb->kgf", t_re, cos_b, preferred_element_type=jnp.float32) + jnp.einsum(
        "kbf,gb->kgf", t_im, sin_b, preferred_element_type=jnp.float32
    )
    c_im = jnp.einsum("kbf,gb->kgf", t_im, cos_b, preferred_element_type=jnp.float32) - jnp.einsum(
        "kbf,gb->kgf", t_re, sin_b, preferred_element_type=jnp.float32
    )
    power = (c_re * c_re + c_im * c_im) * (1.0 / (taps * channels))
    return power.reshape(beams_here, count, channels)


def blocked_power(extended, proto, first, count):
    taps = proto.shape[0]

    def block_power(index):
        start = first + index * PFB_BLK
        window = lax.dynamic_slice_in_dim(extended, start, PFB_BLK + taps - 1, 1)
        return spectra_power(window, proto)

    blocks = lax.map(block_power, jnp.arange(count // PFB_BLK, dtype=jnp.int32))
    beams_here = extended.shape[0]
    return jnp.moveaxis(blocks, 0, 1).reshape(beams_here, count, extended.shape[2])


def fine_masks(groups, width):
    block = jnp.arange(groups, dtype=jnp.int32)[:, None]
    inner = jnp.arange(width, dtype=jnp.int32)[None, :]
    fine = block * FD * (width - 1 - inner) // (groups * (width - 1))
    return jnp.stack([(fine == step).astype(jnp.bfloat16) for step in range(FD)])


def subband_sums(flat_ext, groups, count):
    beams_here, length, channels = flat_ext.shape
    width = channels // NBLK
    view = flat_ext.reshape(beams_here, length, NBLK, width)
    masks = fine_masks(groups, width)
    total = jnp.zeros((beams_here, groups, NBLK, count), jnp.float32)
    for step in range(FD):
        part = view[:, FD - 1 - step : FD - 1 - step + count]
        total = total + jnp.einsum(
            "bkci,gi->bgck", part, masks[step], preferred_element_type=jnp.float32
        )
    return (total * (1.0 / math.sqrt(width))).astype(jnp.bfloat16)


def dedisperse(extended, delays, count):
    length = count + WMAX - 1
    total = 0.0
    for value in range(MAXT + 1):
        start = (MAXT - value) * TT
        window = extended[..., start : start + length]
        mask = (delays == value).astype(jnp.bfloat16)
        total = total + jnp.einsum(
            "rgck,gjc->rgjk", window, mask, preferred_element_type=jnp.float32
        )
    return total * (1.0 / math.sqrt(NBLK))


def boxcar(series, widths, count):
    lags = jnp.arange(WMAX, dtype=jnp.int32)
    weights = (lags[None, :] < widths[:, None]).astype(jnp.float32) / jnp.sqrt(
        widths.astype(jnp.float32)
    )[:, None]
    stacked = jnp.stack(
        [series[..., WMAX - 1 - lag : WMAX - 1 - lag + count] for lag in range(WMAX)], -2
    )
    return jnp.einsum("rgjik,wi->rgjwk", stacked, weights)


def slot_table(owners, owner_count, capacity):
    owner = owners[:, 0]
    groups = owner.shape[0]
    index = jnp.arange(groups, dtype=jnp.int32)
    same = owner[:, None] == owner[None, :]
    earlier = index[None, :] < index[:, None]
    rank = jnp.sum((same & earlier).astype(jnp.int32), 1)
    hit_owner = owner[None, None, :] == jnp.arange(owner_count, dtype=jnp.int32)[:, None, None]
    hit_slot = rank[None, None, :] == jnp.arange(capacity, dtype=jnp.int32)[None, :, None]
    return (hit_owner & hit_slot).astype(jnp.int32)


def shards(raw, proto, delays, widths, owners):
    taps, channels = proto.shape
    beams_here = raw.shape[0]
    spec = raw.shape[1] // channels
    groups = delays.shape[0]
    owner_count = lax.axis_size("dm")
    capacity = 2 * (groups // owner_count)
    halo = MAXT * TT + WMAX - 1
    frames = raw.reshape(beams_here, spec, channels)
    total_spectra = spec * lax.axis_size("tm")
    history = taps - 1 + FD - 1
    before = shifted(frames[:, spec - history :], "tm", 1)
    extended = jnp.concatenate([before, frames], 1)
    early_power = spectra_power(extended[:, 0 : FD - 1 + taps - 1], proto)
    main_power = blocked_power(extended, proto, FD - 1, spec)
    band = lax.psum(jnp.sum(main_power, 1), "tm") / total_spectra
    ratio = jnp.concatenate([early_power, main_power], 1) / (band[:, None, :] + 1e-06)
    flat_ext = (ratio - jnp.mean(ratio, 2, keepdims=True)).astype(jnp.bfloat16)
    sub = subband_sums(flat_ext, groups, spec)
    table = slot_table(owners, owner_count, capacity)
    table_bf = table.astype(jnp.bfloat16)
    packed = jnp.einsum(
        "osg,bgck->obsck", table_bf, sub, preferred_element_type=jnp.float32
    ).astype(jnp.bfloat16)
    received = lax.all_to_all(packed, "dm", split_axis=0, concat_axis=1, tiled=True)[0]
    earlier_sub = shifted(received[..., spec - halo :], "tm", 1)
    owned = jnp.concatenate([earlier_sub, received], -1)
    mine = lax.dynamic_index_in_dim(table, lax.axis_index("dm"), 0, keepdims=False)
    slot_delays = jnp.sum(mine[:, :, None, None] * delays[None], 1)
    series = dedisperse(owned, slot_delays, spec)
    box = boxcar(series, widths, spec).astype(jnp.bfloat16)
    result = jnp.transpose(box, (1, 0, 2, 3, 4))
    return result.reshape(capacity, owner_count, beams_here, result.shape[2], result.shape[3], spec)


def solution(mesh):
    return jax.shard_map(
        shards,
        mesh=mesh,
        in_specs=(P(("group", "dm", "beam"), "tm"), P(), P(), P(), P()),
        out_specs=P("dm", "group", "beam", None, None, "tm"),
        check_vma=False,
    )
```

profile of v0, /device:TPU:0, one launch (start us, length us, event | category | flops | bytes accessed | tf_op | source)
XLA Modules:
  0.0 273.6 jit_solution(5279019373399987779)
XLA Ops:
  6.5 90.0 %reduce.3 = bf16[2097152]{0:T(1024)(128)(2,1)} reduce(bf16[1,2097152]{1,0:T(2,128)(2,1)} %param.7, bf16[]{:T(256)} %constant.179), dimensions={0}, to_apply=%param.7.reduce_sub_computation | reduce | bytes 8388610 | tf_op args[0]
  96.5 7.3 %reshape.370 = bf16[1,128,16384]{2,1,0:T(8,128)(2,1)} reshape(bf16[2097152]{0:T(1024)(128)(2,1)} %reduce.3) | data formatting | bytes 8388608 | tf_op jit(solution)/shard_map/reshape | solution.py:141
  104.9 5.0 %collective-permute-start = (bf16[1,6,16384]{2,1,0:T(8,128)(2,1)S(1)}, bf16[1,6,16384]{2,1,0:T(8,128)(2,1)S(1)}, u32[]{:S(2)}, u32[]{:S(2)}) collective-permute-start(bf16[1,6,16384]{2,1,0:T(8,128)(2,1)S(1)} %slice.160), channel_id=1, source_target_pairs={{0,2},{1,3},{4,6},{5,7},{8,10},{9,11},{12,14},{13,15},{16,18},{17,... | collective-permute-start | bytes 589832 | tf_op jit(solution)/shard_map/ppermute | solution.py:19
  110.6 4.6 %collective-permute-done = bf16[1,6,16384]{2,1,0:T(8,128)(2,1)S(1)} collective-permute-done((bf16[1,6,16384]{2,1,0:T(8,128)(2,1)S(1)}, bf16[1,6,16384]{2,1,0:T(8,128)(2,1)S(1)}, u32[]{:S(2)}, u32[]{:S(2)}) %collective-permute-start) | collective-permute-done | bytes 196640 | tf_op jit(solution)/shard_map/ppermute | solution.py:19
  117.6 5.4 %pad_maximum_fusion = bf16[1,134,16384]{2,1,0:T(8,128)(2,1)} fusion(bf16[1,128,16384]{2,1,0:T(8,128)(2,1)} %reshape.370, bf16[1,6,16384]{2,1,0:T(8,128)(2,1)S(1)} %collective-permute-done), kind=kLoop, calls=%fused_computation.68 | loop fusion | flops 8781824 | bytes 8781824 | tf_op jit(solution)/shard_map/concatenate | solution.py:145
  122.9 75.4 %while.13 = (s32[]{:T(128)}, f32[8,1,16,16384]{3,2,1,0:T(8,128)}, s32[8]{0:T(128)S(1)}, bf16[1,134,16384]{2,1,0:T(8,128)(2,1)}, f32[4,16384]{1,0:T(4,128)S(1)}, ...) while((s32[]{:T(128)}, f32[8,1,16,16384]{3,2,1,0:T(8,128)}, ...), condition=%wide.region_3.4_spmd, body=%wide.region_2.3_spmd.sunk | while | flops 411435008 | bytes 22545144 | solution.py:71
  124.4 3.3 %fusion.264 = bf16[2,8,128,128]{3,1,2,0:T(8,128)(2,1)S(1)} fusion(bf16[1,134,16384]{2,1,0:T(8,128)(2,1)} %get-tuple-element.202, s32[]{:T(128)S(6)} %add.420, s32[]{:T(128)S(6)} %add.421, s32[]{:T(128)S(6)} %add.422, s32[]{:T(128)S(6)} %select_n.191, f32[16384]{0:T(1024)S(1)} %bitcast.245, f32[16384]{0:T(1024)S(1)} %bitcast.246, ...), kind=kLoop, calls=%fused_computation.11.clone.1 | loop fusion | flops 3145728 | bytes 2883600 | tf_op jit(solution)/shard_map/while
  134.1 3.2 %fusion.264 = bf16[2,8,128,128]{3,1,2,0:T(8,128)(2,1)S(1)} fusion(bf16[1,134,16384]{2,1,0:T(8,128)(2,1)} %get-tuple-element.202, s32[]{:T(128)S(6)} %add.420, s32[]{:T(128)S(6)} %add.421, s32[]{:T(128)S(6)} %add.422, s32[]{:T(128)S(6)} %select_n.191, f32[16384]{0:T(1024)S(1)} %bitcast.245, f32[16384]{0:T(1024)S(1)} %bitcast.246, ...), kind=kLoop, calls=%fused_computation.11.clone.1 | loop fusion | flops 3145728 | bytes 2883600 | tf_op jit(solution)/shard_map/while
  143.7 3.0 %fusion.264 = bf16[2,8,128,128]{3,1,2,0:T(8,128)(2,1)S(1)} fusion(bf16[1,134,16384]{2,1,0:T(8,128)(2,1)} %get-tuple-element.202, s32[]{:T(128)S(6)} %add.420, s32[]{:T(128)S(6)} %add.421, s32[]{:T(128)S(6)} %add.422, s32[]{:T(128)S(6)} %select_n.191, f32[16384]{0:T(1024)S(1)} %bitcast.245, f32[16384]{0:T(1024)S(1)} %bitcast.246, ...), kind=kLoop, calls=%fused_computation.11.clone.1 | loop fusion | flops 3145728 | bytes 2883600 | tf_op jit(solution)/shard_map/while
  153.1 3.0 %fusion.264 = bf16[2,8,128,128]{3,1,2,0:T(8,128)(2,1)S(1)} fusion(bf16[1,134,16384]{2,1,0:T(8,128)(2,1)} %get-tuple-element.202, s32[]{:T(128)S(6)} %add.420, s32[]{:T(128)S(6)} %add.421, s32[]{:T(128)S(6)} %add.422, s32[]{:T(128)S(6)} %select_n.191, f32[16384]{0:T(1024)S(1)} %bitcast.245, f32[16384]{0:T(1024)S(1)} %bitcast.246, ...), kind=kLoop, calls=%fused_computation.11.clone.1 | loop fusion | flops 3145728 | bytes 2883600 | tf_op jit(solution)/shard_map/while
  162.5 2.9 %fusion.264 = bf16[2,8,128,128]{3,1,2,0:T(8,128)(2,1)S(1)} fusion(bf16[1,134,16384]{2,1,0:T(8,128)(2,1)} %get-tuple-element.202, s32[]{:T(128)S(6)} %add.420, s32[]{:T(128)S(6)} %add.421, s32[]{:T(128)S(6)} %add.422, s32[]{:T(128)S(6)} %select_n.191, f32[16384]{0:T(1024)S(1)} %bitcast.245, f32[16384]{0:T(1024)S(1)} %bitcast.246, ...), kind=kLoop, calls=%fused_computation.11.clone.1 | loop fusion | flops 3145728 | bytes 2883600 | tf_op jit(solution)/shard_map/while
  171.8 3.0 %fusion.264 = bf16[2,8,128,128]{3,1,2,0:T(8,128)(2,1)S(1)} fusion(bf16[1,134,16384]{2,1,0:T(8,128)(2,1)} %get-tuple-element.202, s32[]{:T(128)S(6)} %add.420, s32[]{:T(128)S(6)} %add.421, s32[]{:T(128)S(6)} %add.422, s32[]{:T(128)S(6)} %select_n.191, f32[16384]{0:T(1024)S(1)} %bitcast.245, f32[16384]{0:T(1024)S(1)} %bitcast.246, ...), kind=kLoop, calls=%fused_computation.11.clone.1 | loop fusion | flops 3145728 | bytes 2883600 | tf_op jit(solution)/shard_map/while
  181.2 2.9 %fusion.264 = bf16[2,8,128,128]{3,1,2,0:T(8,128)(2,1)S(1)} fusion(bf16[1,134,16384]{2,1,0:T(8,128)(2,1)} %get-tuple-element.202, s32[]{:T(128)S(6)} %add.420, s32[]{:T(128)S(6)} %add.421, s32[]{:T(128)S(6)} %add.422, s32[]{:T(128)S(6)} %select_n.191, f32[16384]{0:T(1024)S(1)} %bitcast.245, f32[16384]{0:T(1024)S(1)} %bitcast.246, ...), kind=kLoop, calls=%fused_computation.11.clone.1 | loop fusion | flops 3145728 | bytes 2883600 | tf_op jit(solution)/shard_map/while
  190.5 2.9 %fusion.264 = bf16[2,8,128,128]{3,1,2,0:T(8,128)(2,1)S(1)} fusion(bf16[1,134,16384]{2,1,0:T(8,128)(2,1)} %get-tuple-element.202, s32[]{:T(128)S(6)} %add.420, s32[]{:T(128)S(6)} %add.421, s32[]{:T(128)S(6)} %add.422, s32[]{:T(128)S(6)} %select_n.191, f32[16384]{0:T(1024)S(1)} %bitcast.245, f32[16384]{0:T(1024)S(1)} %bitcast.246, ...), kind=kLoop, calls=%fused_computation.11.clone.1 | loop fusion | flops 3145728 | bytes 2883600 | tf_op jit(solution)/shard_map/while
  198.3 4.5 %reduce_sum.40 = f32[16384]{0:T(1024)} reduce(f32[8,1,16,16384]{3,2,1,0:T(8,128)} %get-tuple-element.95, f32[]{:T(128)} %constant.170.clone.1), dimensions={0,1,2}, to_apply=%region_4.5 | reduce | flops 2080768 | bytes 8454148 | tf_op jit(solution)/shard_map/reduce_sum | solution.py:148
  203.5 6.0 %copy.62 = f32[16,8,64,256]{3,2,1,0:T(8,128)S(1)} copy(f32[16,8,64,256]{3,1,2,0:T(8,128)} %bitcast.241) | data formatting | bytes 16777216
  209.5 8.1 %copy.45 = f32[1,128,64,256]{3,1,2,0:T(8,128)} copy(f32[1,128,64,256]{3,2,1,0:T(8,128)S(1)} %bitcast.243) | data formatting | bytes 16777216 | tf_op jit(solution)/shard_map/concatenate | solution.py:149
  217.6 8.4 %all-reduce.2.cloned.1.call-done = f32[1,16384]{1,0:T(1,128)} async-done(((f32[1,16384]{1,0:T(1,128)}), f32[1,16384]{1,0:T(1,128)}) %all-reduce.2.cloned.1.call-update) | async-done | bytes 65552 | tf_op jit(solution)/shard_map/psum | solution.py:148
  227.0 4.2 %fusion.56 = f32[131]{0:T(256)S(1)} fusion(f32[1,128,16384]{2,1,0:T(8,128)} %bitcast.242, f32[1,3,16384]{2,1,0:T(4,128)S(1)} %concatenate.39, f32[16384]{0:T(1024)S(1)} %bitcast.253), kind=kLoop, calls=%fused_computation.67 | loop fusion | flops 6438781 | bytes 8651276 | tf_op jit(solution)/shard_map/reduce_sum | solution.py:150
  231.3 4.8 %fusion.55 = bf16[1,131,64,256]{3,1,2,0:T(8,128)(2,1)S(1)} fusion(f32[1,128,64,256]{3,1,2,0:T(8,128)} %copy.45, f32[1,3,64,256]{3,1,2,0:T(4,128)S(1)} %copy.44, f32[131]{0:T(256)S(1)} %broadcast_multiply_fusion, f32[64,256]{1,0:T(8,128)S(1)} %add.239), kind=kLoop, calls=%fused_computation.65 | loop fusion | flops 8585216 | bytes 12943884 | tf_op jit(solution)/shard_map/convert_element_type | solution.py:150
  239.7 3.6 %fusion.61 = bf16[4,1,4,64,128]{4,2,0,3,1:T(4,128)(2,1)S(1)} fusion(f32[8,128,64]{1,0,2:T(8,128)S(1)} %fusion.64, bf16[1,131,64,256]{3,1,2,0:T(8,128)(2,1)} %copy-done, s32[256]{0:T(256)S(1)} %iota_subtract_fusion, s32[8]{0:T(128)S(1)} %iota_multiply_fusion.2, pred[4,8]{1,0:T(4,128)(4,1)S(1)} %get-tuple-element.124, pred[4,8]{1,0:T(4,128)(4,1)S(1)} %get-tuple-element.125), kind=kOutput, calls=%fused_computation.78 | convolution fusion | flops 36000128 | bytes 4719712 | tf_op jit(solution)/shard_map/osg,bgck->obsck/dot_general | solution.py:154
  244.1 4.6 %all-to-all-start = ((bf16[4,1,4,64,128]{4,2,3,1,0:T(4,128)(2,1)}), bf16[4,1,4,64,128]{4,2,3,1,0:T(4,128)(2,1)S(1)}, u32[]{:S(2)}, u32[]{:S(2)}) async-start(bf16[4,1,4,64,128]{4,2,3,1,0:T(4,128)(2,1)} %copy.46), calls=%async_computation | async-start | bytes 524288 | tf_op jit(solution)/shard_map/all_to_all | solution.py:157
  248.8 8.4 %all-to-all-done = bf16[4,1,4,64,128]{4,2,3,1,0:T(4,128)(2,1)S(1)} async-done(((bf16[4,1,4,64,128]{4,2,3,1,0:T(4,128)(2,1)}), bf16[4,1,4,64,128]{4,2,3,1,0:T(4,128)(2,1)S(1)}, u32[]{:S(2)}, u32[]{:S(2)}) %all-to-all-start) | async-done | bytes 262176 | tf_op jit(solution)/shard_map/all_to_all | solution.py:157
  259.9 3.8 %collective-permute-done.1 = bf16[4,4,64,31]{3,2,0,1:T(8,128)(2,1)S(1)} collective-permute-done((bf16[4,4,64,31]{3,2,0,1:T(8,128)(2,1)S(1)}, bf16[4,4,64,31]{3,2,0,1:T(8,128)(2,1)S(1)}, u32[]{:S(2)}, u32[]{:S(2)}) %collective-permute-start.1) | collective-permute-done | bytes 63520 | tf_op jit(solution)/shard_map/ppermute | solution.py:19
  (156 shorter events, 61.6 us)
Async XLA Ops:
  6.5 103.7 %copy-start.1 = (f32[4,16384]{1,0:T(4,128)S(1)}, f32[4,16384]{1,0:T(4,128)}, u32[]{:S(2)}) copy-start(f32[4,16384]{1,0:T(4,128)} %param.8) | copy-start | bytes 786436
  6.5 103.9 %copy-start.4 = (s32[8,1]{0,1:T(1,128)S(1)}, s32[8,1]{0,1:T(1,128)}, u32[]{:S(2)}) copy-start(s32[8,1]{0,1:T(1,128)} %param.11) | copy-start | bytes 100
  6.5 219.4 %all-reduce.2.cloned.1.call-start = ((), (), s32[]{:S(2)}) async-start(), calls=%async_computation.1 | async-start | bytes 131072 | tf_op jit(solution)/shard_map/psum | solution.py:148
  104.9 10.4 %collective-permute-start = (bf16[1,6,16384]{2,1,0:T(8,128)(2,1)S(1)}, bf16[1,6,16384]{2,1,0:T(8,128)(2,1)S(1)}, u32[]{:S(2)}, u32[]{:S(2)}) collective-permute-start(bf16[1,6,16384]{2,1,0:T(8,128)(2,1)S(1)} %slice.160), channel_id=1, source_target_pairs={{0,2},{1,3},{4,6},{5,7},{8,10},{9,11},{12,14},{13,15},{16,18},{17,... | collective-permute-start | bytes 589832 | tf_op jit(solution)/shard_map/ppermute | solution.py:19
  236.1 2.4 copy-start
  238.5 10.2 %copy-start.2 = (s32[8,4,64]{2,1,0:T(4,128)S(1)}, s32[8,4,64]{2,1,0:T(4,128)}, u32[]{:S(2)}) copy-start(s32[8,4,64]{2,1,0:T(4,128)} %param.9) | copy-start | bytes 24580
  238.5 10.2 %copy-start.3 = (s32[8]{0:T(128)S(1)}, s32[8]{0:T(128)}, u32[]{:S(2)}) copy-start(s32[8]{0:T(128)} %param.10) | copy-start | bytes 100
  244.1 13.0 %all-to-all-start = ((bf16[4,1,4,64,128]{4,2,3,1,0:T(4,128)(2,1)}), bf16[4,1,4,64,128]{4,2,3,1,0:T(4,128)(2,1)S(1)}, u32[]{:S(2)}, u32[]{:S(2)}) async-start(bf16[4,1,4,64,128]{4,2,3,1,0:T(4,128)(2,1)} %copy.46), calls=%async_computation | async-start | bytes 524288 | tf_op jit(solution)/shard_map/all_to_all | solution.py:157
  257.4 6.3 %collective-permute-start.1 = (bf16[4,4,64,31]{3,2,0,1:T(8,128)(2,1)S(1)}, bf16[4,4,64,31]{3,2,0,1:T(8,128)(2,1)S(1)}, u32[]{:S(2)}, u32[]{:S(2)}) collective-permute-start(bf16[4,4,64,31]{3,2,0,1:T(8,128)(2,1)S(1)} %slice.169), channel_id=1, source_target_pairs={{0,2},{1,3},{4,6},{5,7},{8,10},{9,11},{12,14},{13,15},{16,18},{17,... | collective-permute-start | bytes 190472 | tf_op jit(solution)/shard_map/ppermute | solution.py:19
Sparse Core Ops, SparseCore 0:
  202.9 22.9 all-reduce.1
where the time goes:
time: 274 us
  other arithmetic  137 us (50%)
  local copies, waits for them, and re-layouts  42.6 us (16%)
  matrix products  37.3 us (14%)
  waiting for transfers between devices  25.2 us (9%)
  between operations  13.6 us (5%)
  starting transfers between devices  12.1 us (4%)
  loops' own time  5.67 us (2%)
    unnamed x2, other arithmetic  90.3 us
    while x8, other arithmetic  24.1 us
    dynamic_update_slice x8, local copies, waits for them, and re-layouts, blocked_power(): blocks = lax.map(block_power, jnp.arange(count // PFB_BLK, dtype=jnp.int32))  8.56 us
    psum x1, waiting for transfers between devices, shards(): band = lax.psum(jnp.sum(main_power, 1), 'tm') / total_spectra  8.4 us
    ppermute x2, waiting for transfers between devices, shifted(): lax.ppermute(value, axis, [(source, source + steps) for source in range(f...  8.39 us
    all_to_all x1, waiting for transfers between devices, shards(): lax.all_to_all(packed, 'dm', split_axis=0, concat_axis=1, tiled=True)[0]  8.38 us
    concatenate x4, local copies, waits for them, and re-layouts, shards(): jnp.concatenate([early_power, main_power], 1) / (band[:, None, :] + 1e-06)  8.35 us
    ppermute x2, starting transfers between devices, shifted(): lax.ppermute(value, axis, [(source, source + steps) for source in range(f...  7.52 us
  transfers between devices with their start and end apart: 4, of which 4 were waited for; matrix products, arithmetic and copies ran while one was open for 6% of the time, Pallas kernels for 0%

commit v1 on v0

--- a/solution.py
+++ b/solution.py
@@ -145,7 +145,7 @@
     extended = jnp.concatenate([before, frames], 1)
     early_power = spectra_power(extended[:, 0 : FD - 1 + taps - 1], proto)
     main_power = blocked_power(extended, proto, FD - 1, spec)
-    band = lax.psum(jnp.sum(main_power, 1), "tm") / total_spectra
+    band = jnp.sum(lax.all_gather(jnp.sum(main_power, 1), "tm"), axis=0) / total_spectra
     ratio = jnp.concatenate([early_power, main_power], 1) / (band[:, None, :] + 1e-06)
     flat_ext = (ratio - jnp.mean(ratio, 2, keepdims=True)).astype(jnp.bfloat16)
     sub = subband_sums(flat_ext, groups, spec)

time: 274 us -> 252 us (0.920)
  between operations: 13.6 us -> 0.27 us
  waiting for transfers between devices: 25.2 us -> 15.1 us
  blocking collectives: 0 us -> 5.6 us
  other arithmetic: 137 us -> 133 us
  local copies, waits for them, and re-layouts: 42.6 us -> 39.6 us
    psum x1 -> x0, waiting for transfers between devices: 8.4 us -> none  [shards(): band = lax.psum(jnp.sum(main_power, 1), 'tm') / total_spectra]
    all_gather x0 -> x1, blocking collectives: none -> 5.6 us  [shards(): lax.all_gather(jnp.sum(main_power, 1), 'tm')]
    concatenate x4, local copies, waits for them, and re-layouts: 8.35 us -> 5.14 us  [shards(): jnp.concatenate([early_power, main_power], 1) / (band[:, None, :] + 1e-06)]
  transfers between devices with their start and end apart: 4 -> 3, of which waited for: 4 -> 3; matrix products, arithmetic and copies ran while one was open for 6% -> 0% of each run, Pallas kernels for 0% -> 0%
where the time goes in v1:
time: 252 us; the launch traced here: 251 us
  other arithmetic  133 us (53%)
  local copies, waits for them, and re-layouts  39.6 us (16%)
  matrix products  37.3 us (15%)
  waiting for transfers between devices  15.1 us (6%)
  starting transfers between devices  13.9 us (6%)
  loops' own time  6.16 us (2%)
  blocking collectives  5.6 us (2%)
    unnamed x2, other arithmetic  90.3 us
    while x8, other arithmetic  23.8 us
    ppermute x2, starting transfers between devices, shifted(): lax.ppermute(value, axis, [(source, source + steps) for source in range(f...  9.01 us
    dynamic_update_slice x8, local copies, waits for them, and re-layouts, blocked_power(): blocks = lax.map(block_power, jnp.arange(count // PFB_BLK, dtype=jnp.int32))  8.55 us
    ppermute x2, waiting for transfers between devices, shifted(): lax.ppermute(value, axis, [(source, source + steps) for source in range(f...  8.39 us
    reshape x1, local copies, waits for them, and re-layouts, shards(): frames = raw.reshape(beams_here, spec, channels)  7.31 us
    all_to_all x1, waiting for transfers between devices, shards(): lax.all_to_all(packed, 'dm', split_axis=0, concat_axis=1, tiled=True)[0]  6.71 us
    unnamed x19, local copies, waits for them, and re-layouts  6.65 us
  transfers between devices with their start and end apart: 3, of which 3 were waited for; matrix products, arithmetic and copies ran while one was open for 0% of the time, Pallas kernels for 0%

profile of v1, /device:TPU:0, one launch (start us, length us, event | category | flops | bytes accessed | tf_op | source)
XLA Modules:
  0.0 251.0 jit_solution(14337672699493932852)
XLA Ops:
  0.0 90.0 %reduce.5 = bf16[2097152]{0:T(1024)(128)(2,1)} reduce(bf16[1,2097152]{1,0:T(2,128)(2,1)} %param.7, bf16[]{:T(256)} %constant.179), dimensions={0}, to_apply=%param.7.reduce_sub_computation | reduce | bytes 8388610 | tf_op args[0]
  90.0 7.3 %reshape.375 = bf16[1,128,16384]{2,1,0:T(8,128)(2,1)} reshape(bf16[2097152]{0:T(1024)(128)(2,1)} %reduce.5) | data formatting | bytes 8388608 | tf_op jit(solution)/shard_map/reshape | solution.py:141
  98.3 5.0 %collective-permute-start = (bf16[1,6,16384]{2,1,0:T(8,128)(2,1)S(1)}, bf16[1,6,16384]{2,1,0:T(8,128)(2,1)S(1)}, u32[]{:S(2)}, u32[]{:S(2)}) collective-permute-start(bf16[1,6,16384]{2,1,0:T(8,128)(2,1)S(1)} %slice.160), channel_id=1, source_target_pairs={{0,2},{1,3},{4,6},{5,7},{8,10},{9,11},{12,14},{13,15},{16,18},{17,... | collective-permute-start | bytes 589832 | tf_op jit(solution)/shard_map/ppermute | solution.py:19
  104.1 4.6 %collective-permute-done = bf16[1,6,16384]{2,1,0:T(8,128)(2,1)S(1)} collective-permute-done((bf16[1,6,16384]{2,1,0:T(8,128)(2,1)S(1)}, bf16[1,6,16384]{2,1,0:T(8,128)(2,1)S(1)}, u32[]{:S(2)}, u32[]{:S(2)}) %collective-permute-start) | collective-permute-done | bytes 196640 | tf_op jit(solution)/shard_map/ppermute | solution.py:19
  111.6 5.3 %pad_maximum_fusion = bf16[1,134,16384]{2,1,0:T(8,128)(2,1)} fusion(bf16[1,128,16384]{2,1,0:T(8,128)(2,1)} %reshape.375, bf16[1,6,16384]{2,1,0:T(8,128)(2,1)S(1)} %collective-permute-done), kind=kLoop, calls=%fused_computation.68 | loop fusion | flops 8781824 | bytes 8781824 | tf_op jit(solution)/shard_map/concatenate | solution.py:145
  116.9 75.7 %while.13 = (s32[]{:T(128)}, f32[8,1,16,16384]{3,2,1,0:T(8,128)}, s32[8]{0:T(128)S(1)}, bf16[1,134,16384]{2,1,0:T(8,128)(2,1)}, f32[4,16384]{1,0:T(4,128)S(1)}, ...) while((s32[]{:T(128)}, f32[8,1,16,16384]{3,2,1,0:T(8,128)}, ...), condition=%wide.region_3.4_spmd, body=%wide.region_2.3_spmd.sunk | while | flops 411435008 | bytes 22545144 | solution.py:71
  118.5 3.1 %fusion.263 = bf16[2,8,128,128]{3,1,2,0:T(8,128)(2,1)S(1)} fusion(bf16[1,134,16384]{2,1,0:T(8,128)(2,1)} %get-tuple-element.200, s32[]{:T(128)S(6)} %add.407, s32[]{:T(128)S(6)} %add.408, s32[]{:T(128)S(6)} %add.409, s32[]{:T(128)S(6)} %select_n.191, f32[16384]{0:T(1024)S(1)} %bitcast.243, f32[16384]{0:T(1024)S(1)} %bitcast.244, ...), kind=kLoop, calls=%fused_computation.11.clone.1 | loop fusion | flops 3145728 | bytes 2883600 | tf_op jit(solution)/shard_map/while
  128.1 3.2 %fusion.263 = bf16[2,8,128,128]{3,1,2,0:T(8,128)(2,1)S(1)} fusion(bf16[1,134,16384]{2,1,0:T(8,128)(2,1)} %get-tuple-element.200, s32[]{:T(128)S(6)} %add.407, s32[]{:T(128)S(6)} %add.408, s32[]{:T(128)S(6)} %add.409, s32[]{:T(128)S(6)} %select_n.191, f32[16384]{0:T(1024)S(1)} %bitcast.243, f32[16384]{0:T(1024)S(1)} %bitcast.244, ...), kind=kLoop, calls=%fused_computation.11.clone.1 | loop fusion | flops 3145728 | bytes 2883600 | tf_op jit(solution)/shard_map/while
  137.8 3.0 %fusion.263 = bf16[2,8,128,128]{3,1,2,0:T(8,128)(2,1)S(1)} fusion(bf16[1,134,16384]{2,1,0:T(8,128)(2,1)} %get-tuple-element.200, s32[]{:T(128)S(6)} %add.407, s32[]{:T(128)S(6)} %add.408, s32[]{:T(128)S(6)} %add.409, s32[]{:T(128)S(6)} %select_n.191, f32[16384]{0:T(1024)S(1)} %bitcast.243, f32[16384]{0:T(1024)S(1)} %bitcast.244, ...), kind=kLoop, calls=%fused_computation.11.clone.1 | loop fusion | flops 3145728 | bytes 2883600 | tf_op jit(solution)/shard_map/while
  147.3 2.9 %fusion.263 = bf16[2,8,128,128]{3,1,2,0:T(8,128)(2,1)S(1)} fusion(bf16[1,134,16384]{2,1,0:T(8,128)(2,1)} %get-tuple-element.200, s32[]{:T(128)S(6)} %add.407, s32[]{:T(128)S(6)} %add.408, s32[]{:T(128)S(6)} %add.409, s32[]{:T(128)S(6)} %select_n.191, f32[16384]{0:T(1024)S(1)} %bitcast.243, f32[16384]{0:T(1024)S(1)} %bitcast.244, ...), kind=kLoop, calls=%fused_computation.11.clone.1 | loop fusion | flops 3145728 | bytes 2883600 | tf_op jit(solution)/shard_map/while
  156.6 2.9 %fusion.263 = bf16[2,8,128,128]{3,1,2,0:T(8,128)(2,1)S(1)} fusion(bf16[1,134,16384]{2,1,0:T(8,128)(2,1)} %get-tuple-element.200, s32[]{:T(128)S(6)} %add.407, s32[]{:T(128)S(6)} %add.408, s32[]{:T(128)S(6)} %add.409, s32[]{:T(128)S(6)} %select_n.191, f32[16384]{0:T(1024)S(1)} %bitcast.243, f32[16384]{0:T(1024)S(1)} %bitcast.244, ...), kind=kLoop, calls=%fused_computation.11.clone.1 | loop fusion | flops 3145728 | bytes 2883600 | tf_op jit(solution)/shard_map/while
  166.0 3.0 %fusion.263 = bf16[2,8,128,128]{3,1,2,0:T(8,128)(2,1)S(1)} fusion(bf16[1,134,16384]{2,1,0:T(8,128)(2,1)} %get-tuple-element.200, s32[]{:T(128)S(6)} %add.407, s32[]{:T(128)S(6)} %add.408, s32[]{:T(128)S(6)} %add.409, s32[]{:T(128)S(6)} %select_n.191, f32[16384]{0:T(1024)S(1)} %bitcast.243, f32[16384]{0:T(1024)S(1)} %bitcast.244, ...), kind=kLoop, calls=%fused_computation.11.clone.1 | loop fusion | flops 3145728 | bytes 2883600 | tf_op jit(solution)/shard_map/while
  175.5 2.8 %fusion.263 = bf16[2,8,128,128]{3,1,2,0:T(8,128)(2,1)S(1)} fusion(bf16[1,134,16384]{2,1,0:T(8,128)(2,1)} %get-tuple-element.200, s32[]{:T(128)S(6)} %add.407, s32[]{:T(128)S(6)} %add.408, s32[]{:T(128)S(6)} %add.409, s32[]{:T(128)S(6)} %select_n.191, f32[16384]{0:T(1024)S(1)} %bitcast.243, f32[16384]{0:T(1024)S(1)} %bitcast.244, ...), kind=kLoop, calls=%fused_computation.11.clone.1 | loop fusion | flops 3145728 | bytes 2883600 | tf_op jit(solution)/shard_map/while
  184.8 2.9 %fusion.263 = bf16[2,8,128,128]{3,1,2,0:T(8,128)(2,1)S(1)} fusion(bf16[1,134,16384]{2,1,0:T(8,128)(2,1)} %get-tuple-element.200, s32[]{:T(128)S(6)} %add.407, s32[]{:T(128)S(6)} %add.408, s32[]{:T(128)S(6)} %add.409, s32[]{:T(128)S(6)} %select_n.191, f32[16384]{0:T(1024)S(1)} %bitcast.243, f32[16384]{0:T(1024)S(1)} %bitcast.244, ...), kind=kLoop, calls=%fused_computation.11.clone.1 | loop fusion | flops 3145728 | bytes 2883600 | tf_op jit(solution)/shard_map/while
  192.7 3.9 %reduce_sum.47 = f32[16384]{0:T(1024)S(1)} reduce(f32[8,1,16,16384]{3,2,1,0:T(8,128)} %get-tuple-element.95, f32[]{:T(128)} %constant.170.clone.1), dimensions={0,1,2}, to_apply=%region_4.5 | reduce | flops 2080768 | bytes 8454148 | tf_op jit(solution)/shard_map/reduce_sum | solution.py:148
  196.5 5.6 %all-gather = f32[32768]{0:T(1024)S(1)} all-gather(f32[16384]{0:T(1024)S(1)} %reduce_sum.47), channel_id=2, replica_groups=mesh['group'=2,'dm'=4,'tm'=2,'beam'=2] {'tm'}, dimensions={0}, use_global_device_ids=true | all-gather | bytes 196608 | tf_op jit(solution)/shard_map/all_gather | solution.py:148
  202.4 4.2 %fusion.56 = f32[131]{0:T(256)S(1)} fusion(f32[1,128,16384]{2,1,0:T(8,128)} %bitcast.239, f32[1,3,16384]{2,1,0:T(4,128)S(1)} %concatenate.39, f32[16384]{0:T(1024)S(1)} %multiply_add_fusion), kind=kLoop, calls=%fused_computation.67 | loop fusion | flops 6438781 | bytes 8651276 | tf_op jit(solution)/shard_map/reduce_sum | solution.py:150
  206.8 6.0 %copy.62 = f32[16,8,64,256]{3,2,1,0:T(8,128)S(1)} copy(f32[16,8,64,256]{3,1,2,0:T(8,128)} %bitcast.240) | data formatting | bytes 16777216
  212.8 4.9 %copy.45 = f32[1,128,64,256]{3,1,2,0:T(8,128)S(1)} copy(f32[1,128,64,256]{3,2,1,0:T(8,128)S(1)} %bitcast.241) | data formatting | bytes 16777216 | tf_op jit(solution)/shard_map/concatenate | solution.py:149
  223.9 3.6 %fusion.61 = bf16[4,1,4,64,128]{4,2,0,3,1:T(4,128)(2,1)S(1)} fusion(f32[8,128,64]{1,0,2:T(8,128)S(1)} %fusion.64, bf16[1,131,64,256]{3,1,2,0:T(8,128)(2,1)} %copy-done, s32[256]{0:T(256)S(1)} %iota_subtract_fusion, s32[8]{0:T(128)S(1)} %iota_multiply_fusion.2, pred[4,8]{1,0:T(4,128)(4,1)S(1)} %get-tuple-element.122, pred[4,8]{1,0:T(4,128)(4,1)S(1)} %get-tuple-element.123), kind=kOutput, calls=%fused_computation.78 | convolution fusion | flops 36000128 | bytes 4719712 | tf_op jit(solution)/shard_map/osg,bgck->obsck/dot_general | solution.py:154
  228.2 4.9 %all-to-all-start = ((bf16[4,1,4,64,128]{4,2,3,1,0:T(4,128)(2,1)}), bf16[4,1,4,64,128]{4,2,3,1,0:T(4,128)(2,1)S(1)}, u32[]{:S(2)}, u32[]{:S(2)}) async-start(bf16[4,1,4,64,128]{4,2,3,1,0:T(4,128)(2,1)} %copy.46), calls=%async_computation | async-start | bytes 524288 | tf_op jit(solution)/shard_map/all_to_all | solution.py:157
  233.2 6.7 %all-to-all-done = bf16[4,1,4,64,128]{4,2,3,1,0:T(4,128)(2,1)S(1)} async-done(((bf16[4,1,4,64,128]{4,2,3,1,0:T(4,128)(2,1)}), bf16[4,1,4,64,128]{4,2,3,1,0:T(4,128)(2,1)S(1)}, u32[]{:S(2)}, u32[]{:S(2)}) %all-to-all-start) | async-done | bytes 262176 | tf_op jit(solution)/shard_map/all_to_all | solution.py:157
  240.1 4.0 %collective-permute-start.1 = (bf16[4,4,64,31]{3,2,0,1:T(8,128)(2,1)S(1)}, bf16[4,4,64,31]{3,2,0,1:T(8,128)(2,1)S(1)}, u32[]{:S(2)}, u32[]{:S(2)}) collective-permute-start(bf16[4,4,64,31]{3,2,0,1:T(8,128)(2,1)S(1)} %slice.169), channel_id=1, source_target_pairs={{0,2},{1,3},{4,6},{5,7},{8,10},{9,11},{12,14},{13,15},{16,18},{17,... | collective-permute-start | bytes 190472 | tf_op jit(solution)/shard_map/ppermute | solution.py:19
  244.1 3.8 %collective-permute-done.1 = bf16[4,4,64,31]{3,2,0,1:T(8,128)(2,1)S(1)} collective-permute-done((bf16[4,4,64,31]{3,2,0,1:T(8,128)(2,1)S(1)}, bf16[4,4,64,31]{3,2,0,1:T(8,128)(2,1)S(1)}, u32[]{:S(2)}, u32[]{:S(2)}) %collective-permute-start.1) | collective-permute-done | bytes 63520 | tf_op jit(solution)/shard_map/ppermute | solution.py:19
  (156 shorter events, 61.0 us)
Async XLA Ops:
  0.0 103.7 %copy-start.1 = (f32[4,16384]{1,0:T(4,128)S(1)}, f32[4,16384]{1,0:T(4,128)}, u32[]{:S(2)}) copy-start(f32[4,16384]{1,0:T(4,128)} %param.8) | copy-start | bytes 786436
  0.0 103.9 %copy-start.4 = (s32[8,1]{0,1:T(1,128)S(1)}, s32[8,1]{0,1:T(1,128)}, u32[]{:S(2)}) copy-start(s32[8,1]{0,1:T(1,128)} %param.11) | copy-start | bytes 100
  98.3 10.4 %collective-permute-start = (bf16[1,6,16384]{2,1,0:T(8,128)(2,1)S(1)}, bf16[1,6,16384]{2,1,0:T(8,128)(2,1)S(1)}, u32[]{:S(2)}, u32[]{:S(2)}) collective-permute-start(bf16[1,6,16384]{2,1,0:T(8,128)(2,1)S(1)} %slice.160), channel_id=1, source_target_pairs={{0,2},{1,3},{4,6},{5,7},{8,10},{9,11},{12,14},{13,15},{16,18},{17,... | collective-permute-start | bytes 589832 | tf_op jit(solution)/shard_map/ppermute | solution.py:19
  220.2 2.4 copy-start
  222.6 10.5 %copy-start.2 = (s32[8,4,64]{2,1,0:T(4,128)S(1)}, s32[8,4,64]{2,1,0:T(4,128)}, u32[]{:S(2)}) copy-start(s32[8,4,64]{2,1,0:T(4,128)} %param.9) | copy-start | bytes 24580
  222.7 10.5 %copy-start.3 = (s32[8]{0:T(128)S(1)}, s32[8]{0:T(128)}, u32[]{:S(2)}) copy-start(s32[8]{0:T(128)} %param.10) | copy-start | bytes 100
  228.2 11.6 %all-to-all-start = ((bf16[4,1,4,64,128]{4,2,3,1,0:T(4,128)(2,1)}), bf16[4,1,4,64,128]{4,2,3,1,0:T(4,128)(2,1)S(1)}, u32[]{:S(2)}, u32[]{:S(2)}) async-start(bf16[4,1,4,64,128]{4,2,3,1,0:T(4,128)(2,1)} %copy.46), calls=%async_computation | async-start | bytes 524288 | tf_op jit(solution)/shard_map/all_to_all | solution.py:157
  240.1 7.8 %collective-permute-start.1 = (bf16[4,4,64,31]{3,2,0,1:T(8,128)(2,1)S(1)}, bf16[4,4,64,31]{3,2,0,1:T(8,128)(2,1)S(1)}, u32[]{:S(2)}, u32[]{:S(2)}) collective-permute-start(bf16[4,4,64,31]{3,2,0,1:T(8,128)(2,1)S(1)} %slice.169), channel_id=1, source_target_pairs={{0,2},{1,3},{4,6},{5,7},{8,10},{9,11},{12,14},{13,15},{16,18},{17,... | collective-permute-start | bytes 190472 | tf_op jit(solution)/shard_map/ppermute | solution.py:19
